TPU v7x, 512 devices: a whole 4x8x8 slice. The times are simulated.
512 devices in a mesh: frame: 64 (over z, x, core), segment: 8 (over y).
Axes of the slice: x: 4, y: 8, z: 8, core: 2. Of those that a mesh axis runs over, the one named last changes fastest.
Arguments:
- state: bfloat16 [8, 2048, 3072], P('segment', 'frame'), may hold values from -6 to 6
- modulation: float32 [8, 32, 7, 3072], P('segment'), may hold values from -3 to 3
- noise_level: int32 [8], replicated, may hold values from 0 to 31
- frame_mask: int32 [8, 8], replicated, may hold values from 0 to 1, as said below
- offset: int32 [1], replicated, may hold values from 1 to 7
Outputs:
- next_state: bfloat16 [8, 2048, 3072], P('segment', 'frame')
Inputs may be any that keep to these rules, and one draw needn't show every extreme that they name: frame_mask[i, i] is 1 and frame_mask[i, j] is 0 for j > i.
All inputs are finite; a program needn't handle non-finite values.
Results may differ from a plain program's by a relative error of at most 0.017.
Values may be sent and summed in bfloat16 or wider, within the bound.
No kernel may reach another device: no remote copies, remote signals or barrier semaphores. Data moves between devices by JAX's collectives and lax.ppermute only.
A program may use at most 128 MiB of HBM per device.

v0:
```python
import math

import jax
import jax.numpy as jnp
from jax import lax
from jax.sharding import PartitionSpec as P

HEAD = 128
FRAME_TOK = 256


epsilon = 1e-06
negative = -1e30


def side_by_side(arrays, axis, dim, along):
    both = jnp.concatenate(arrays, axis=along)
    whole, at, finished = (lax.all_gather(both, axis, axis=dim, tiled=True), 0, [])
    for a in arrays:
        finished.append(lax.slice_in_dim(whole, at, at + a.shape[along], axis=along))
        at += a.shape[along]
    return tuple(finished)


def passed_along(shard, axis, by):
    peers = lax.axis_size(axis)
    return lax.ppermute(shard, axis, [(i, (i + by) % peers) for i in range(peers)])


def normalize(values):
    widened = values.astype(jnp.float32)
    square_mean = jnp.mean(widened * widened, axis=-1, keepdims=True)
    return (widened * lax.rsqrt(square_mean + epsilon)).astype(jnp.bfloat16)


def modulate(normed, modifiers, column):
    scaled = (
        normed.astype(jnp.float32) * (1.0 + modifiers[..., column, :])
        + modifiers[..., column + 1, :]
    )
    return scaled.astype(jnp.bfloat16)


def body(state, modulation, noise_level, frame_mask, offset):
    hidden = state[0]
    level_table = modulation[0]
    tok_rows, model_width = hidden.shape
    head_count = model_width // HEAD
    devices = lax.axis_size("frame")
    position = lax.axis_index("frame")
    frame_span = FRAME_TOK // tok_rows
    span_bits = frame_span.bit_length() - 1
    bit_total = devices.bit_length() - 1
    frame_mods = jnp.take(level_table, noise_level, axis=0)
    own_frame = position // frame_span
    own_mods = lax.dynamic_index_in_dim(frame_mods, own_frame, 0, keepdims=False)
    normed = normalize(hidden)
    queries = modulate(normed, own_mods, 0)
    query_sets = ((queries, own_frame),)
    prepared = []
    rows_given, frame_given = query_sets[0]
    mask_row = lax.dynamic_index_in_dim(frame_mask, frame_given, 0, keepdims=False)
    prepared.append((rows_given.reshape(rows_given.shape[0], head_count, HEAD), mask_row))
    scale_factor = 1.0 / math.sqrt(HEAD)
    block_rows = 512

    def frames_of(first_row, rows_here):
        return (
            first_row + tok_rows * jnp.arange(rows_here // tok_rows, dtype=jnp.int32)
        ) // FRAME_TOK

    def attend(running, key_rows, value_rows, shard_frames):
        rows_here = key_rows.shape[0]
        key_heads = key_rows.reshape(rows_here, head_count, HEAD)
        value_heads = value_rows.reshape(rows_here, head_count, HEAD)
        updated = []
        for (query_heads, mask_row), state_now in zip(prepared, running):
            shard_allowed = jnp.take(mask_row, shard_frames) == 1
            allowed = jnp.broadcast_to(
                shard_allowed[:, None], (shard_frames.shape[0], tok_rows)
            ).reshape(rows_here)

            def update(previous, query_heads=query_heads, allowed=allowed):
                run_max, denominator, accumulated = previous
                scores = (
                    jnp.einsum(
                        "thd,rhd->htr", query_heads, key_heads, preferred_element_type=jnp.float32
                    )
                    * scale_factor
                )
                scores = jnp.where(allowed[None, None, :], scores, negative)
                new_max = jnp.maximum(run_max, jnp.max(scores, axis=-1))
                weights = jnp.where(
                    allowed[None, None, :], jnp.exp(scores - new_max[..., None]), 0.0
                ).astype(jnp.bfloat16)
                factor = jnp.exp(run_max - new_max)
                denominator = denominator * factor + jnp.sum(weights.astype(jnp.float32), axis=-1)
                accumulated = accumulated * factor[..., None] + jnp.einsum(
                    "htr,rhd->htd", weights, value_heads, preferred_element_type=jnp.float32
                )
                return (new_max, denominator, accumulated)

            updated.append(
                lax.cond(jnp.any(shard_allowed), update, lambda previous: previous, state_now)
            )
        return tuple(updated)

    initial = tuple(
        (
            (
                jnp.full((head_count, heads_given.shape[0]), negative, jnp.float32),
                jnp.zeros((head_count, heads_given.shape[0]), jnp.float32),
                jnp.zeros((head_count, heads_given.shape[0], HEAD), jnp.float32),
            )
            for heads_given, _unused in prepared
        )
    )
    own_keys = modulate(normed, own_mods, 2)
    own_values = modulate(normed, own_mods, 4)

    def consume_ready(carried, block_pieces, block_start):
        rows_here = block_pieces[0].shape[0]
        return attend(carried, block_pieces[0], block_pieces[1], frames_of(block_start, rows_here))

    running = initial
    pieces = side_by_side((own_keys, own_values), "frame", 0, 1)
    rows_here = pieces[0].shape[0]
    block_count = rows_here // block_rows
    stacked = tuple((member.reshape(block_count, block_rows, member.shape[1]) for member in pieces))
    starts = block_rows * jnp.arange(block_count, dtype=jnp.int32)

    def advance(carried, block_item):
        return (consume_ready(carried, block_item[0], block_item[1]), None)

    running, _unused = lax.scan(advance, running, (stacked, starts))
    results = []
    for run_max, denominator, accumulated in running:
        merged = accumulated / denominator[..., None]
        results.append(
            jnp.transpose(merged, (1, 0, 2))
            .reshape(merged.shape[1], model_width)
            .astype(jnp.bfloat16)
        )
    attention = results[0]
    section_rows = (
        hidden.astype(jnp.float32) + own_mods[6] * attention.astype(jnp.float32)
    ).astype(jnp.bfloat16)
    passed = passed_along(section_rows, "segment", 1)
    distance = (devices - offset[0] * frame_span % devices) % devices
    rolled = passed
    for bit_index in range(span_bits, bit_total):
        shifted = passed_along(rolled, "frame", 1 << bit_index)
        rolled = jnp.where(distance >> bit_index & 1 == 1, shifted, rolled)
    finished = jnp.where(lax.axis_index("segment") == 0, rolled, passed)
    return finished[None]


def solution(mesh):
    return jax.shard_map(
        body,
        mesh=mesh,
        in_specs=(P("segment", "frame", None), P("segment", None, None, None), P(), P(), P()),
        out_specs=P("segment", "frame", None),
        check_vma=False,
    )
```

profile of v0, /device:TPU:32, one launch (start us, length us, event | category | flops | bytes accessed | tf_op | source)
XLA Modules:
  0.0 294.1 jit_solution(13320497735180953602)
XLA Ops:
  6.5 0.7 compare_and_fusion
  7.2 0.7 compare_select_fusion.8
  7.9 3.4 %copy.26 = f32[1,32,7,3072]{3,2,1,0:T(8,128)S(1)} copy(f32[1,32,7,3072]{3,1,2,0:T(8,128)} %param.10) | data formatting | bytes 5505024 | tf_op args[1]
  11.3 0.6 dynamic-slice
  11.9 1.5 gather_fusion.1
  13.4 1.6 dynamic-slice_select_fusion
  15.4 0.8 pad_maximum_fusion
  16.4 0.2 add_convert_fusion
  16.6 131.5 %all-gather.2.cloned.1.call-done = bf16[2048,6144]{1,0:T(8,128)(2,1)} async-done(((bf16[32,6144]{1,0:T(8,128)(2,1)}), bf16[2048,6144]{1,0:T(8,128)(2,1)}) %all-gather.2.cloned.1.call-update) | async-done | bytes 25165840 | tf_op jit(solution)/shard_map/all_gather | solution.py:18
  148.1 17.6 %fusion.17 = (bf16[2048,3072]{1,0:T(8,128)(2,1)}, bf16[2048,3072]{1,0:T(8,128)(2,1)}) fusion(bf16[2048,6144]{1,0:T(8,128)(2,1)} %all-gather.2.cloned.1.call-done), kind=kLoop, calls=%fused_computation.66 | loop fusion | bytes 50331648 | tf_op jit(solution)/shard_map/slice | solution.py:20
  165.7 16.7 %copy.12 = bf16[4,512,3072]{1,2,0:T(8,128)(2,1)} copy(bf16[4,512,3072]{2,1,0:T(8,128)(2,1)} %bitcast.80) | data formatting | bytes 25165824 | tf_op jit(solution)/shard_map/while | solution.py:135
  182.3 16.7 %copy.13 = bf16[4,512,3072]{1,2,0:T(8,128)(2,1)} copy(bf16[4,512,3072]{2,1,0:T(8,128)(2,1)} %bitcast.79) | data formatting | bytes 25165824 | tf_op jit(solution)/shard_map/while | solution.py:135
  199.1 24.5 %while.16 = (s32[]{:T(128)}, f32[24,32]{1,0:T(8,128)S(1)}, f32[24,32]{1,0:T(8,128)S(1)}, f32[24,32,128]{2,1,0:T(8,128)S(1)}, s32[4]{0:T(128)S(1)}, /*index=5*/s3...) while((s32[]{:T(128)}, f32[24,32]{1,0:T(8,128)S(1)}, ...), condition=%wide.region_7.8_spmd, body=%wide.region_1.0_spmd.sunk | while | flops 205852272 | bytes 24633340 | solution.py:135
  199.1 0.6 dynamic_slice.42
  199.7 0.6 fusion.23
  200.4 0.7 gather_fusion
  201.0 0.6 compare_select_fusion.10
  201.7 1.3 compare_reduce_fusion.2
  203.7 5.9 %conditional.2 = ((f32[24,32]{1,0:T(8,128)S(1)}, f32[24,32]{1,0:T(8,128)S(1)}, f32[24,32,128]{2,1,0:T(8,128)S(1)})) conditional(s32[]{:T(128)} %convert_element_type.143, (f32[24,32]{1,0:T(8,128)S(1)}, f32[24,32]{1,0:T(8,128)S(1)}, f32[24,32,128]{2,1,0:T(8,128)S(1)}) %tuple.53, (s32[16,1]{0,1:T(1,128)S(1)}, s32[16,1]{0,1:T(1,128)S(1)}, ...), branch_computations={%region_3.3_spmd, %region_4.6_spmd} | conditional | flops 205850192 | bytes 24628484 | solution.py:104
  203.9 3.3 %constant_dynamic-slice_fusion = (bf16[1,512,3072]{1,2,0:T(8,128)(2,1)S(1)}, bf16[1,512,3072]{1,2,0:T(8,128)(2,1)S(1)}) fusion(bf16[4,512,3072]{1,2,0:T(8,128)(2,1)} %get-tuple-element.231, s32[]{:T(128)} %get-tuple-element.227, bf16[4,512,3072]{1,2,0:T(8,128)(2,1)} %get-tuple-element.226), kind=kLoop, calls=%fused_computation.14 | loop fusion | bytes 12582916 | tf_op jit(solution)/shard_map/while/body/jit(dynamic_index_in_dim)/dynamic_slice | solution.py:135
  207.1 0.7 bitcast_reduce_fusion
  207.8 0.5 convert_reduce_fusion
  208.3 1.3 convolution_add_fusion
  209.6 0.6 dynamic_slice.42
  210.3 0.6 fusion.23
  210.9 0.7 gather_fusion
  211.6 0.6 compare_select_fusion.10
  212.2 1.3 compare_reduce_fusion.2
  214.3 0.6 dynamic_slice.42
  214.9 0.6 fusion.23
  215.6 0.7 gather_fusion
  216.2 0.6 compare_select_fusion.10
  216.9 1.3 compare_reduce_fusion.2
  218.9 0.6 dynamic_slice.42
  219.6 0.6 fusion.23
  220.2 0.7 gather_fusion
  220.9 0.6 compare_select_fusion.10
  221.5 1.3 compare_reduce_fusion.2
  223.6 0.2 fusion.15
  223.8 2.5 collective-permute-start
  226.3 7.7 %collective-permute-done = bf16[32,3072]{1,0:T(8,128)(2,1)S(1)} collective-permute-done((bf16[32,3072]{1,0:T(8,128)(2,1)S(1)}, bf16[32,3072]{1,0:T(8,128)(2,1)S(1)}, u32[]{:S(2)}, u32[]{:S(2)}) %collective-permute-start) | collective-permute-done | bytes 196640 | tf_op jit(solution)/shard_map/ppermute | solution.py:27
  233.9 1.9 collective-permute-start.1
  236.5 22.8 %collective-permute-done.1 = bf16[32,3072]{1,0:T(8,128)(2,1)S(1)} collective-permute-done((bf16[32,3072]{1,0:T(8,128)(2,1)S(1)}, bf16[32,3072]{1,0:T(8,128)(2,1)S(1)}, u32[]{:S(2)}, u32[]{:S(2)}) %collective-permute-start.1) | collective-permute-done | bytes 196640 | tf_op jit(solution)/shard_map/ppermute | solution.py:27
  259.3 1.9 collective-permute-start.2
  261.3 11.6 %collective-permute-done.2 = bf16[32,3072]{1,0:T(8,128)(2,1)S(1)} collective-permute-done((bf16[32,3072]{1,0:T(8,128)(2,1)S(1)}, bf16[32,3072]{1,0:T(8,128)(2,1)S(1)}, u32[]{:S(2)}, u32[]{:S(2)}) %collective-permute-start.2) | collective-permute-done | bytes 196640 | tf_op jit(solution)/shard_map/ppermute | solution.py:27
  272.9 2.4 collective-permute-start.3
  275.3 11.2 %collective-permute-done.3 = bf16[32,3072]{1,0:T(8,128)(2,1)S(1)} collective-permute-done((bf16[32,3072]{1,0:T(8,128)(2,1)S(1)}, bf16[32,3072]{1,0:T(8,128)(2,1)S(1)}, u32[]{:S(2)}, u32[]{:S(2)}) %collective-permute-start.3) | collective-permute-done | bytes 196640 | tf_op jit(solution)/shard_map/ppermute | solution.py:27
  286.5 0.7 select_bitcast_fusion
  (39 shorter events, 0.9 us)
Async XLA Ops:
  6.5 9.8 %copy-start = (s32[8,8]{1,0:T(8,128)S(1)}, s32[8,8]{1,0:T(8,128)}, u32[]{:S(2)}) copy-start(s32[8,8]{1,0:T(8,128)} %param.12) | copy-start | bytes 772
  6.5 141.6 %all-gather.2.cloned.1.call-start = ((), (), s32[]{:S(2)}) async-start(), calls=%async_computation | async-start | bytes 25559040 | tf_op jit(solution)/shard_map/all_gather | solution.py:18
  7.9 7.2 %copy-start.2 = (bf16[1,32,3072]{2,1,0:T(8,128)(2,1)S(1)}, bf16[1,32,3072]{2,1,0:T(8,128)(2,1)}, u32[]{:S(2)}) copy-start(bf16[1,32,3072]{2,1,0:T(8,128)(2,1)} %param.9) | copy-start | bytes 589828
  223.6 63.7 %copy-start.1 = (s32[8,8]{1,0:T(8,128)S(1)}, s32[8,8]{1,0:T(8,128)}, u32[]{:S(2)}) copy-start(s32[8,8]{1,0:T(8,128)} %param.12) | copy-start | bytes 772
  223.8 10.2 %collective-permute-start = (bf16[32,3072]{1,0:T(8,128)(2,1)S(1)}, bf16[32,3072]{1,0:T(8,128)(2,1)S(1)}, u32[]{:S(2)}, u32[]{:S(2)}) collective-permute-start(bf16[32,3072]{1,0:T(8,128)(2,1)S(1)} %fusion.15), channel_id=1, source_target_pairs={{0,1},{1,2},{2,3},{3,4},{4,5},{5,6},{6,7},{7,0},{8,9},{9,10},{10,1... | collective-permute-start | bytes 589832 | tf_op jit(solution)/shard_map/ppermute | solution.py:27
  233.9 25.4 %collective-permute-start.1 = (bf16[32,3072]{1,0:T(8,128)(2,1)S(1)}, bf16[32,3072]{1,0:T(8,128)(2,1)S(1)}, u32[]{:S(2)}, u32[]{:S(2)}) collective-permute-start(bf16[32,3072]{1,0:T(8,128)(2,1)S(1)} %collective-permute-done), channel_id=1, source_target_pairs={{0,64},{8,72},{16,80},{24,88},{32,96},{40,104},{48,112},{56,120},{... | collective-permute-start | bytes 589832 | tf_op jit(solution)/shard_map/ppermute | solution.py:27
  259.3 13.6 %collective-permute-start.2 = (bf16[32,3072]{1,0:T(8,128)(2,1)S(1)}, bf16[32,3072]{1,0:T(8,128)(2,1)S(1)}, u32[]{:S(2)}, u32[]{:S(2)}) collective-permute-start(bf16[32,3072]{1,0:T(8,128)(2,1)S(1)} %broadcast_select_fusion), channel_id=1, source_target_pairs={{0,128},{8,136},{16,144},{24,152},{32,160},{40,168},{48,176},{56,1... | collective-permute-start | bytes 589832 | tf_op jit(solution)/shard_map/ppermute | solution.py:27
  272.9 13.6 %collective-permute-start.3 = (bf16[32,3072]{1,0:T(8,128)(2,1)S(1)}, bf16[32,3072]{1,0:T(8,128)(2,1)S(1)}, u32[]{:S(2)}, u32[]{:S(2)}) collective-permute-start(bf16[32,3072]{1,0:T(8,128)(2,1)S(1)} %broadcast_select_fusion.1), channel_id=1, source_target_pairs={{0,256},{8,264},{16,272},{24,280},{32,288},{40,296},{48,304},{56,3... | collective-permute-start | bytes 589832 | tf_op jit(solution)/shard_map/ppermute | solution.py:27
Sparse Core Ops, SparseCore 0:
  16.3 131.7 all-gather.1
where the time goes:
time: 295 us; the launch traced here: 294 us
  waiting for transfers between devices  185 us (63%)
  local copies, waits for them, and re-layouts  65.2 us (22%)
  other arithmetic  16.2 us (5%)
  between operations  14.3 us (5%)
  starting transfers between devices  8.69 us (3%)
  loops' own time  3.03 us (1%)
    all_gather x1, waiting for transfers between devices, side_by_side(): lax.all_gather(both, axis, axis=dim, tiled=True)  132 us
    ppermute x4, waiting for transfers between devices, passed_along(): lax.ppermute(shard, axis, [(i, (i + by) % peers) for i in range(peers)])  53.3 us
    while x2, local copies, waits for them, and re-layouts, body(): running, _unused = lax.scan(advance, running, (stacked, starts))  33.3 us
    slice x1, local copies, waits for them, and re-layouts, side_by_side(): lax.slice_in_dim(whole, at, at + a.shape[along], axis=along)  17.6 us
    ppermute x4, starting transfers between devices, passed_along(): lax.ppermute(shard, axis, [(i, (i + by) % peers) for i in range(peers)])  8.69 us
  transfers between devices with their start and end apart: 5, of which 5 were waited for; matrix products, arithmetic and copies ran while one was open for 0% of the time, Pallas kernels for 0%

commit v1 on v0

v1 whole, which is shorter than its diff:
```python
import math

import jax
import jax.numpy as jnp
from jax import lax
from jax.experimental import pallas as pl
from jax.experimental.pallas import tpu as pltpu
from jax.sharding import PartitionSpec as P

HEAD = 128
HEADS = 24
WIDTH = HEAD * HEADS
FRAMES = 8
ROWS = 32
SLOT = ROWS + 8
CHIPS = 32
PER_FRAME = CHIPS // FRAMES
HALF = PER_FRAME * ROWS
COLUMNS = 7

epsilon = 1e-06
negative = -1e30

VMEM = pl.BlockSpec(memory_space=pltpu.VMEM)
SMEM = pl.BlockSpec(memory_space=pltpu.SMEM)
ANY = pl.BlockSpec(memory_space=pl.ANY)


def pack_kernel(state, packed):
    wide = state[...].astype(jnp.float32)
    factor = lax.rsqrt(jnp.sum(wide * wide, axis=-1, keepdims=True) * (1.0 / WIDTH) + epsilon)
    high = factor.astype(jnp.bfloat16).astype(jnp.float32)
    middle = (factor - high).astype(jnp.bfloat16).astype(jnp.float32)
    low = factor - high - middle
    lane = lax.broadcasted_iota(jnp.int32, (8, HEAD), 1)
    factors = jnp.zeros((8, HEAD), jnp.float32)
    for group in range(ROWS // 8):
        for at, piece in enumerate((high, middle, low)):
            rows = jnp.broadcast_to(piece[8 * group : 8 * group + 8], (8, HEAD))
            factors = jnp.where(lane == 32 * group + at, rows, factors)
    for two in range(HEADS // 2):
        a, b = 2 * two, 2 * two + 1
        packed[2 * SLOT * two : 2 * SLOT * (two + 1), :] = jnp.concatenate(
            [
                wide[:, HEAD * a : HEAD * (a + 1)],
                factors,
                wide[:, HEAD * b : HEAD * (b + 1)],
                factors,
            ],
            axis=0,
        ).astype(jnp.bfloat16)
    packed[HEADS * SLOT :, :] = jnp.zeros(((CHIPS - HEADS) * SLOT, HEAD), jnp.bfloat16)


def pick_kernel(levels, table, mods, column, sem):
    head = jnp.minimum(lax.axis_index("frame") // 2, HEADS - 1)
    copy = pltpu.make_async_copy(
        table.at[:, :, pl.ds(pl.multiple_of(head * HEAD, HEAD), HEAD)], column, sem
    )
    copy.start()
    copy.wait()
    for frame in range(FRAMES):
        level = levels[frame]
        for c in range(COLUMNS):
            mods[8 * frame + c : 8 * frame + c + 1, :] = column[c, pl.ds(level, 1), :]


def unpacked(chunk):
    wide = chunk.astype(jnp.float32)
    state, factor = [], []
    for slot in range(PER_FRAME):
        at = SLOT * slot
        state.append(wide[at : at + ROWS])
        pieces = wide[at + ROWS : at + SLOT]
        for group in range(ROWS // 8):
            lane = 32 * group
            whole = (
                pieces[:, lane : lane + 1] + pieces[:, lane + 1 : lane + 2]
            ) + pieces[:, lane + 2 : lane + 3]
            factor.append(jnp.broadcast_to(whole, (8, HEAD)))
    state = jnp.concatenate(state, axis=0)
    normed = (state * jnp.concatenate(factor, axis=0)).astype(jnp.bfloat16)
    return state, normed.astype(jnp.float32)


def attend_kernel(offset, mask, mods, slots, out, keys, values, queries, kept, scores):
    core = lax.rem(lax.axis_index("frame"), 2)
    last = lax.axis_index("segment") == lax.axis_size("segment") - 1
    shift = jnp.where(last, offset[0], 0)
    ones = jnp.ones((16, 2 * HALF), jnp.bfloat16)

    def rows_of(frame, c):
        return mods[8 * frame + c : 8 * frame + c + 1, :]

    for frame in range(FRAMES):
        for part in range(2):
            at = CHIPS * SLOT * part + PER_FRAME * SLOT * frame
            _unused, normed = unpacked(slots[at : at + PER_FRAME * SLOT, :])
            key = normed * (1.0 + rows_of(frame, 2)) + rows_of(frame, 3)
            value = normed * (1.0 + rows_of(frame, 4)) + rows_of(frame, 5)
            row = 2 * HALF * frame + HALF * part
            keys[row : row + HALF, :] = key.astype(jnp.bfloat16)
            values[frame, :HEAD, HALF * part : HALF * (part + 1)] = value.T.astype(jnp.bfloat16)
        values[frame, HEAD:, :] = ones
        at = pl.multiple_of(CHIPS * SLOT * core + PER_FRAME * SLOT * frame, 16)
        state, normed = unpacked(slots[pl.ds(at, PER_FRAME * SLOT), :])
        query = normed * (1.0 + rows_of(frame, 0)) + rows_of(frame, 1)
        side = HALF * (frame % 2)
        queries[frame // 2, :, side : side + HALF] = query.T.astype(jnp.bfloat16)
        kept[HALF * frame : HALF * (frame + 1), :] = state

    side = lax.broadcasted_iota(jnp.int32, (1, 2 * HALF), 1) < HALF
    rate = math.log2(math.e) / math.sqrt(HEAD)
    for two in range(FRAMES // 2):
        first, second = 2 * two, 2 * two + 1
        query = queries[two]
        top = jnp.full((8, 2 * HALF), negative, jnp.float32)
        for frame in range(second + 1):
            barred = jnp.where(
                side,
                jnp.where(mask[first, frame] == 1, 0.0, negative),
                jnp.where(mask[second, frame] == 1, 0.0, negative),
            )
            here = slice(2 * HALF * frame, 2 * HALF * (frame + 1))
            got = jnp.dot(keys[here, :], query, preferred_element_type=jnp.float32) + barred
            scores[here, :] = got
            top = jnp.maximum(top, jnp.max(got.reshape(2 * HALF // 8, 8, 2 * HALF), axis=0))
        top = jnp.max(top, axis=0, keepdims=True)
        total = jnp.zeros((HEAD + 16, 2 * HALF), jnp.float32)
        for frame in range(second + 1):
            here = slice(2 * HALF * frame, 2 * HALF * (frame + 1))
            weights = jnp.exp2((scores[here, :] - top) * rate).astype(jnp.bfloat16)
            total = total + jnp.dot(values[frame], weights, preferred_element_type=jnp.float32)
        attention = total[:HEAD] * (1.0 / total[HEAD : HEAD + 1])
        attention = attention.astype(jnp.bfloat16).astype(jnp.float32).T
        for frame in (first, second):
            rows = attention[HALF * (frame - first) : HALF * (frame - first + 1)]
            updated = kept[HALF * frame : HALF * (frame + 1), :] + rows_of(frame, 6) * rows
            to = pl.multiple_of(HALF * lax.rem(frame + FRAMES - shift, FRAMES), HALF)
            out[pl.ds(to, HALF), :] = updated.astype(jnp.bfloat16)


def body(state, modulation, noise_level, frame_mask, offset):
    segments = lax.axis_size("segment")
    table = jnp.transpose(modulation[0], (1, 0, 2))
    same_core = [[2 * chip + core for chip in range(CHIPS)] for core in range(2)]
    same_chip = [[2 * chip, 2 * chip + 1] for chip in range(CHIPS)]

    packed = pl.pallas_call(
        pack_kernel,
        out_shape=jax.ShapeDtypeStruct((CHIPS * SLOT, HEAD), jnp.bfloat16),
        in_specs=[VMEM],
        out_specs=VMEM,
        compiler_params=pltpu.CompilerParams(vmem_limit_bytes=8 * 2**20),
        name="pack",
    )(state[0])
    mods = pl.pallas_call(
        pick_kernel,
        out_shape=jax.ShapeDtypeStruct((8 * FRAMES, HEAD), jnp.float32),
        in_specs=[SMEM, ANY],
        out_specs=VMEM,
        scratch_shapes=[
            pltpu.VMEM((COLUMNS, modulation.shape[1], HEAD), jnp.float32),
            pltpu.SemaphoreType.DMA,
        ],
        compiler_params=pltpu.CompilerParams(vmem_limit_bytes=8 * 2**20),
        name="pick",
    )(noise_level, table)
    heads = lax.all_to_all(packed, "frame", 0, 0, axis_index_groups=same_core, tiled=True)
    slots = lax.all_gather(heads, "frame", axis=0, tiled=True, axis_index_groups=same_chip)
    done = pl.pallas_call(
        attend_kernel,
        out_shape=jax.ShapeDtypeStruct((CHIPS * ROWS, HEAD), jnp.bfloat16),
        in_specs=[SMEM, SMEM, VMEM, VMEM],
        out_specs=VMEM,
        scratch_shapes=[
            pltpu.VMEM((FRAMES * 2 * HALF, HEAD), jnp.bfloat16),
            pltpu.VMEM((FRAMES, HEAD + 16, 2 * HALF), jnp.bfloat16),
            pltpu.VMEM((FRAMES // 2, HEAD, 2 * HALF), jnp.bfloat16),
            pltpu.VMEM((FRAMES * HALF, HEAD), jnp.float32),
            pltpu.VMEM((FRAMES * 2 * HALF, 2 * HALF), jnp.float32),
        ],
        compiler_params=pltpu.CompilerParams(vmem_limit_bytes=24 * 2**20),
        name="attend",
    )(offset, frame_mask, mods, slots)
    back = lax.all_to_all(done, "frame", 0, 0, axis_index_groups=same_core, tiled=True)
    rows = jnp.transpose(back[: HEADS * ROWS].reshape(HEADS, ROWS, HEAD), (1, 0, 2))
    passed = lax.ppermute(
        rows.reshape(ROWS, WIDTH), "segment", [(i, (i + 1) % segments) for i in range(segments)]
    )
    return passed[None]


def solution(mesh):
    return jax.shard_map(
        body,
        mesh=mesh,
        in_specs=(P("segment", "frame", None), P("segment", None, None, None), P(), P(), P()),
        out_specs=P("segment", "frame", None),
        check_vma=False,
    )
```

time: 295 us -> 62.1 us (0.21)
  waiting for transfers between devices: 185 us -> 16.5 us
  local copies, waits for them, and re-layouts: 65.2 us -> 4.05 us
  blocking collectives: 0 us -> 19.5 us
  other arithmetic: 16.2 us -> 0 us
  between operations: 14.3 us -> 0.7 us
  starting transfers between devices: 8.69 us -> 15.8 us
  Pallas kernels: 0 us -> 5.37 us
  loops' own time: 3.03 us -> 0 us
    all_gather x1 -> x0, waiting for transfers between devices: 132 us -> none  [side_by_side(): lax.all_gather(both, axis, axis=dim, tiled=True)]
    ppermute x4 -> x1, waiting for transfers between devices: 53.3 us -> 6.18 us  [body(): lax.ppermute(rows.reshape(ROWS, WIDTH), 'segment', [(i, (i + 1) % segment...]
    while x2 -> x0, local copies, waits for them, and re-layouts: 33.3 us -> none  [body(): running, _unused = lax.scan(advance, running, (stacked, starts))]
    slice x1 -> x0, local copies, waits for them, and re-layouts: 17.6 us -> none  [side_by_side(): lax.slice_in_dim(whole, at, at + a.shape[along], axis=along)]
    all_to_all x0 -> x1, blocking collectives: none -> 17.2 us  [body(): lax.all_to_all(done, 'frame', 0, 0, axis_index_groups=same_core, tiled=True)]
    all_to_all x0 -> x1, starting transfers between devices: none -> 13.2 us  [body(): lax.all_to_all(packed, 'frame', 0, 0, axis_index_groups=same_core, tiled=...]
    all_to_all x0 -> x1, waiting for transfers between devices: none -> 10.3 us  [body(): lax.all_to_all(packed, 'frame', 0, 0, axis_index_groups=same_core, tiled=...]
    select_n x12 -> x0, other arithmetic: 7.33 us -> none  [the longest x8 5.08 us: attend(): shard_allowed = jnp.take(mask_row, shard_frames) == 1]
  transfers between devices with their start and end apart: 5 -> 2, of which waited for: 5 -> 2; matrix products, arithmetic and copies ran while one was open for 0% -> 0% of each run, Pallas kernels for 0% -> 1%
where the time goes in v1:
time: 62.1 us; the launch traced here: 61.8 us
  blocking collectives  19.5 us (31%)
  waiting for transfers between devices  16.5 us (27%)
  starting transfers between devices  15.8 us (25%)
  Pallas kernels  5.37 us (9%)
  local copies, waits for them, and re-layouts  4.05 us (7%)
  between operations  0.7 us (1%)
    all_to_all x1, blocking collectives, body(): lax.all_to_all(done, 'frame', 0, 0, axis_index_groups=same_core, tiled=True)  17.2 us
    all_to_all x1, starting transfers between devices, body(): lax.all_to_all(packed, 'frame', 0, 0, axis_index_groups=same_core, tiled=...  13.2 us
    all_to_all x1, waiting for transfers between devices, body(): lax.all_to_all(packed, 'frame', 0, 0, axis_index_groups=same_core, tiled=...  10.3 us
    ppermute x1, waiting for transfers between devices, body(): lax.ppermute(rows.reshape(ROWS, WIDTH), 'segment', [(i, (i + 1) % segment...  6.18 us
    unnamed x9, local copies, waits for them, and re-layouts  4.03 us
    pallas_call x1, Pallas kernels, body(): pl.pallas_call(attend_kernel, out_shape=jax.ShapeDtypeStruct((CHIPS * ROW...  3.86 us
    ppermute x1, starting transfers between devices, body(): lax.ppermute(rows.reshape(ROWS, WIDTH), 'segment', [(i, (i + 1) % segment...  2.59 us
    all_gather x1, blocking collectives, body(): lax.all_gather(heads, 'frame', axis=0, tiled=True, axis_index_groups=same...  2.26 us
  transfers between devices with their start and end apart: 2, of which 2 were waited for; matrix products, arithmetic and copies ran while one was open for 0% of the time, Pallas kernels for 1%

profile of v1, /device:TPU:32, one launch (start us, length us, event | category | flops | bytes accessed | tf_op | source)
XLA Modules:
  0.0 61.8 jit_solution(17684714692573377473)
XLA Ops:
  0.0 0.0 copy-start.1
  0.0 0.9 %copy-done.1 = bf16[1,32,3072]{2,1,0:T(8,128)(2,1)S(1)} copy-done((bf16[1,32,3072]{2,1,0:T(8,128)(2,1)S(1)}, bf16[1,32,3072]{2,1,0:T(8,128)(2,1)}, u32[]{:S(2)}) %copy-start.1) | copy-done | bytes 196632
  0.9 0.0 copy-start.2
  0.9 0.9 %pack.1 = bf16[1280,128]{1,0:T(8,128)(2,1)} custom-call(bf16[32,3072]{1,0:T(8,128)(2,1)S(1)} %bitcast.16), custom_call_target="tpu_custom_call" | custom-call | tf_op jit(solution)/shard_map/pack/pallas_call | solution.py:149
  1.8 13.2 %all-to-all-start = ((bf16[32,40,128]{2,1,0:T(8,128)(2,1)}), bf16[32,40,128]{2,1,0:T(8,128)(2,1)S(1)}, u32[]{:S(2)}, u32[]{:S(2)}) async-start(bf16[32,40,128]{2,1,0:T(8,128)(2,1)} %bitcast.3), calls=%async_computation | async-start | bytes 655360 | tf_op jit(solution)/shard_map/all_to_all | solution.py:169
  15.6 0.0 copy-start
  15.7 1.8 %copy-done = f32[1,32,7,3072]{3,1,2,0:T(8,128)S(1)} copy-done((f32[1,32,7,3072]{3,1,2,0:T(8,128)S(1)}, f32[1,32,7,3072]{3,1,2,0:T(8,128)}, u32[]{:S(2)}) %copy-start) | copy-done | bytes 2752536
  17.4 0.0 copy-start.3
  17.4 0.7 %copy-done.3 = s32[8]{0:T(128)S(1)} copy-done((s32[8]{0:T(128)S(1)}, s32[8]{0:T(128)}, u32[]{:S(2)}) %copy-start.3) | copy-done | bytes 56
  18.1 0.6 pick.1.mods
  18.7 10.3 %all-to-all-done = bf16[32,40,128]{2,1,0:T(8,128)(2,1)S(1)} async-done(((bf16[32,40,128]{2,1,0:T(8,128)(2,1)}), bf16[32,40,128]{2,1,0:T(8,128)(2,1)S(1)}, u32[]{:S(2)}, u32[]{:S(2)}) %all-to-all-start) | async-done | bytes 327712 | tf_op jit(solution)/shard_map/all_to_all | solution.py:169
  29.0 2.3 %all_gather.3.slots = bf16[2560,128]{1,0:T(8,128)(2,1)S(1)} all-gather(bf16[1280,128]{1,0:T(8,128)(2,1)S(1)} %bitcast.17), channel_id=1, replica_groups={{0,8},{16,24},{32,40},{48,56},{64,72},{80,88},{96,104},{112,120},{128,1..., dimensions={0}, use_global_device_ids=true | all-gather | bytes 983040 | tf_op jit(solution)/shard_map/all_gather | solution.py:170
  31.3 0.0 copy-done.2
  31.3 3.9 %attend.1 = bf16[1024,128]{1,0:T(8,128)(2,1)S(1)} custom-call(s32[1]{0:T(128)S(6)} %copy.10.offset, s32[8,8]{1,0:T(8,128)S(1)} %copy-done.2, f32[64,128]{1,0:T(8,128)S(1)} %pick.1.mods, bf16[2560,128]{1,0:T(8,128)(2,1)S(1)} %all_gather.3.slots), custom_call_target="tpu_custom_call" | custom-call | tf_op jit(solution)/shard_map/attend/pallas_call | solution.py:171
  35.1 17.2 %all_to_all.21 = bf16[32,32,128]{2,1,0:T(8,128)(2,1)S(1)} all-to-all(bf16[32,32,128]{2,1,0:T(8,128)(2,1)S(1)} %bitcast.15), channel_id=1, replica_groups={{0,16,32,48,64,80,96,112,128,144,160,176,192,208,224,240,256,272,288,30..., dimensions={0} | all-to-all | bytes 524288 | tf_op jit(solution)/shard_map/all_to_all | solution.py:186
  52.4 2.6 %collective-permute-start = (bf16[32,3072]{1,0:T(8,128)(2,1)S(1)}, bf16[32,3072]{1,0:T(8,128)(2,1)S(1)}, u32[]{:S(2)}, u32[]{:S(2)}) collective-permute-start(bf16[32,3072]{1,0:T(8,128)(2,1)S(1)} %copy_bitcast_fusion), channel_id=1, source_target_pairs={{0,1},{1,2},{2,3},{3,4},{4,5},{5,6},{6,7},{7,0},{8,9},{9,10},{10,1... | collective-permute-start | bytes 589832 | tf_op jit(solution)/shard_map/ppermute | solution.py:188
  55.0 6.2 %collective-permute-done = bf16[32,3072]{1,0:T(8,128)(2,1)S(1)} collective-permute-done((bf16[32,3072]{1,0:T(8,128)(2,1)S(1)}, bf16[32,3072]{1,0:T(8,128)(2,1)S(1)}, u32[]{:S(2)}, u32[]{:S(2)}) %collective-permute-start) | collective-permute-done | bytes 196640 | tf_op jit(solution)/shard_map/ppermute | solution.py:188
  61.1 0.7 %copy.11 = bf16[1,32,3072]{2,1,0:T(8,128)(2,1)} copy(bf16[1,32,3072]{2,1,0:T(8,128)(2,1)S(1)} %bitcast.18) | data formatting | bytes 393216
  (1 shorter events, 0.0 us)
Async XLA Ops:
  0.0 0.9 %copy-start.1 = (bf16[1,32,3072]{2,1,0:T(8,128)(2,1)S(1)}, bf16[1,32,3072]{2,1,0:T(8,128)(2,1)}, u32[]{:S(2)}) copy-start(bf16[1,32,3072]{2,1,0:T(8,128)(2,1)} %param.5) | copy-start | bytes 589828
  0.9 30.3 %copy-start.2 = (s32[8,8]{1,0:T(8,128)S(1)}, s32[8,8]{1,0:T(8,128)}, u32[]{:S(2)}) copy-start(s32[8,8]{1,0:T(8,128)} %mask.1) | copy-start | bytes 772
  1.8 27.2 %all-to-all-start = ((bf16[32,40,128]{2,1,0:T(8,128)(2,1)}), bf16[32,40,128]{2,1,0:T(8,128)(2,1)S(1)}, u32[]{:S(2)}, u32[]{:S(2)}) async-start(bf16[32,40,128]{2,1,0:T(8,128)(2,1)} %bitcast.3), calls=%async_computation | async-start | bytes 655360 | tf_op jit(solution)/shard_map/all_to_all | solution.py:169
  15.6 1.8 %copy-start = (f32[1,32,7,3072]{3,1,2,0:T(8,128)S(1)}, f32[1,32,7,3072]{3,1,2,0:T(8,128)}, u32[]{:S(2)}) copy-start(f32[1,32,7,3072]{3,1,2,0:T(8,128)} %param.6) | copy-start | bytes 8257540
  17.4 0.7 %copy-start.3 = (s32[8]{0:T(128)S(1)}, s32[8]{0:T(128)}, u32[]{:S(2)}) copy-start(s32[8]{0:T(128)} %levels.1) | copy-start | bytes 100
  52.4 8.8 %collective-permute-start = (bf16[32,3072]{1,0:T(8,128)(2,1)S(1)}, bf16[32,3072]{1,0:T(8,128)(2,1)S(1)}, u32[]{:S(2)}, u32[]{:S(2)}) collective-permute-start(bf16[32,3072]{1,0:T(8,128)(2,1)S(1)} %copy_bitcast_fusion), channel_id=1, source_target_pairs={{0,1},{1,2},{2,3},{3,4},{4,5},{5,6},{6,7},{7,0},{8,9},{9,10},{10,1... | collective-permute-start | bytes 589832 | tf_op jit(solution)/shard_map/ppermute | solution.py:188

commit v2 on v1

v2 whole, which is shorter than its diff:
```python
import math

import jax
import jax.numpy as jnp
from jax import lax
from jax.experimental import pallas as pl
from jax.experimental.pallas import tpu as pltpu
from jax.sharding import PartitionSpec as P

HEAD = 128
HEADS = 24
WIDTH = HEAD * HEADS
FRAMES = 8
ROWS = 32
SLOT = ROWS + 8
CHIPS = 32
PER_FRAME = CHIPS // FRAMES
HALF = PER_FRAME * ROWS
COLUMNS = 7

epsilon = 1e-06
negative = -1e30

VMEM = pl.BlockSpec(memory_space=pltpu.VMEM)
SMEM = pl.BlockSpec(memory_space=pltpu.SMEM)
ANY = pl.BlockSpec(memory_space=pl.ANY)


def pack_kernel(state, packed):
    wide = state[...].astype(jnp.float32)
    factor = lax.rsqrt(jnp.sum(wide * wide, axis=-1, keepdims=True) * (1.0 / WIDTH) + epsilon)
    high = factor.astype(jnp.bfloat16).astype(jnp.float32)
    middle = (factor - high).astype(jnp.bfloat16).astype(jnp.float32)
    low = factor - high - middle
    lane = lax.broadcasted_iota(jnp.int32, (8, HEAD), 1)
    factors = jnp.zeros((8, HEAD), jnp.float32)
    for group in range(ROWS // 8):
        for at, piece in enumerate((high, middle, low)):
            rows = jnp.broadcast_to(piece[8 * group : 8 * group + 8], (8, HEAD))
            factors = jnp.where(lane == 32 * group + at, rows, factors)
    for two in range(CHIPS // 2):
        pieces = []
        for slot in (2 * two, 2 * two + 1):
            chip = PER_FRAME * (FRAMES - 1 - slot // PER_FRAME) + slot % PER_FRAME
            head = min(chip, HEADS - 1)
            pieces += [wide[:, HEAD * head : HEAD * (head + 1)], factors]
        both = jnp.concatenate(pieces, axis=0)
        packed[2 * SLOT * two : 2 * SLOT * (two + 1), :] = both.astype(jnp.bfloat16)


def pick_kernel(levels, table, mods, column, sem):
    head = jnp.minimum(lax.axis_index("frame") // 2, HEADS - 1)
    copy = pltpu.make_async_copy(
        table.at[:, :, pl.ds(pl.multiple_of(head * HEAD, HEAD), HEAD)], column, sem
    )
    copy.start()
    copy.wait()
    for frame in range(FRAMES):
        level = levels[frame]
        for c in range(COLUMNS):
            mods[8 * frame + c : 8 * frame + c + 1, :] = column[c, pl.ds(level, 1), :]


def attend_kernel(
    offset, mask, mods, slots, out, factors, normed, keys, values, queries, scores
):
    core = lax.rem(lax.axis_index("frame"), 2)
    last = lax.axis_index("segment") == lax.axis_size("segment") - 1
    shift = jnp.where(last, offset[0], 0)
    chunk = PER_FRAME * SLOT

    def rows_of(frame, c):
        return mods[8 * frame + c : 8 * frame + c + 1, :]

    quarter = lax.broadcasted_iota(jnp.int32, (HEAD, HEAD), 0) >> 5
    spread = jnp.concatenate(
        [jnp.where(quarter == group, 1.0, 0.0) for group in range(ROWS // 8)], axis=1
    ).astype(jnp.bfloat16)
    for part in range(2):
        pieces = []
        for frame in range(FRAMES):
            at = CHIPS * SLOT * part + chunk * (FRAMES - 1 - frame)
            wide = slots[at : at + chunk, :].astype(jnp.float32)
            for slot in range(PER_FRAME):
                pieces.append(wide[SLOT * slot + ROWS : SLOT * (slot + 1)])
        pieces = jnp.concatenate(pieces, axis=0).astype(jnp.bfloat16)
        factors[part] = jnp.dot(pieces, spread, preferred_element_type=jnp.float32)

    def state_of(wide):
        return jnp.concatenate(
            [wide[SLOT * slot : SLOT * slot + ROWS] for slot in range(PER_FRAME)], axis=0
        )

    def prepare(frame):
        for part in range(2):
            at = CHIPS * SLOT * part + chunk * (FRAMES - 1 - frame)
            state = state_of(slots[at : at + chunk, :].astype(jnp.float32))
            factor = jnp.concatenate(
                [
                    factors[
                        part,
                        8 * (PER_FRAME * frame + slot) : 8 * (PER_FRAME * frame + slot + 1),
                        HEAD * group : HEAD * (group + 1),
                    ]
                    for slot in range(PER_FRAME)
                    for group in range(ROWS // 8)
                ],
                axis=0,
            )
            even = (state * factor).astype(jnp.bfloat16).astype(jnp.float32)
            normed[part, HALF * frame : HALF * (frame + 1), :] = even
            key = even * (1.0 + rows_of(frame, 2)) + rows_of(frame, 3)
            value = even * (1.0 + rows_of(frame, 4)) + rows_of(frame, 5)
            row = 2 * HALF * frame + HALF * part
            keys[row : row + HALF, :] = key.astype(jnp.bfloat16)
            values[frame, :HEAD, HALF * part : HALF * (part + 1)] = value.astype(jnp.bfloat16).T
        values[frame, HEAD:, :] = jnp.ones((16, 2 * HALF), jnp.bfloat16)
        even = normed[core, HALF * frame : HALF * (frame + 1), :]
        query = even * (1.0 + rows_of(frame, 0)) + rows_of(frame, 1)
        half = HALF * (frame % 2)
        queries[frame // 2, :, half : half + HALF] = query.astype(jnp.bfloat16).T

    side = lax.broadcasted_iota(jnp.int32, (1, 2 * HALF), 1) < HALF
    rate = math.log2(math.e) / math.sqrt(HEAD)
    wide = 2 * HALF
    scored, weighed = {}, {}

    def score(two, frame):
        barred = jnp.where(
            side,
            jnp.where(mask[2 * two, frame] == 1, 0.0, negative),
            jnp.where(mask[2 * two + 1, frame] == 1, 0.0, negative),
        )
        got = jnp.dot(
            keys[wide * frame : wide * (frame + 1), :],
            queries[two],
            preferred_element_type=jnp.float32,
        )
        scores[two * (two + 1) + frame] = got
        high = jnp.max(got.reshape(wide // 8, 8, wide), axis=0) + barred
        top, bars = scored.get(two, (None, []))
        scored[two] = (high if top is None else jnp.maximum(top, high), [*bars, barred])

    def weigh(two, frame):
        top, bars = scored[two]
        if frame == 0:
            top = jnp.max(top, axis=0, keepdims=True)
            scored[two] = (top, bars)
        less = top - bars[frame]
        weights = jnp.exp2((scores[two * (two + 1) + frame] - less) * rate)
        part = jnp.dot(
            values[frame], weights.astype(jnp.bfloat16), preferred_element_type=jnp.float32
        )
        weighed[two] = part if frame == 0 else weighed[two] + part

    def finish(two):
        total = weighed.pop(two)
        attention = total[:HEAD] * (1.0 / total[HEAD : HEAD + 1])
        attention = attention.astype(jnp.bfloat16).astype(jnp.float32).T
        for side_of, frame in enumerate((2 * two, 2 * two + 1)):
            at = pl.multiple_of(CHIPS * SLOT * core + chunk * (FRAMES - 1 - frame), 16)
            state = state_of(slots[pl.ds(at, chunk), :].astype(jnp.float32))
            rows = attention[HALF * side_of : HALF * (side_of + 1)]
            to = FRAMES - 1 - lax.rem(frame + FRAMES - shift, FRAMES)
            to = pl.multiple_of(HALF * to, HALF)
            out[pl.ds(to, HALF), :] = (state + rows_of(frame, 6) * rows).astype(jnp.bfloat16)

    for frame in range(FRAMES):
        prepare(frame)
        if frame >= 2:
            two = frame // 2 - 1
            for other in range(two + 1):
                score(two, other + (frame % 2) * (two + 1))
    last_pair = FRAMES // 2 - 1
    steps = [(score, last_pair, other) for other in range(FRAMES)]
    for two in reversed(range(last_pair)):
        for frame in range(2 * two + 2):
            if steps:
                step, pair, other = steps.pop(0)
                step(pair, other)
            weigh(two, frame)
        finish(two)
    for frame in range(FRAMES):
        weigh(last_pair, frame)
    finish(last_pair)


def body(state, modulation, noise_level, frame_mask, offset):
    segments = lax.axis_size("segment")
    table = jnp.transpose(modulation[0], (1, 0, 2))
    same_core = [
        [2 * (PER_FRAME * frame + x) + core for frame in reversed(range(FRAMES)) for x in range(PER_FRAME)]
        for core in range(2)
    ]
    same_chip = [[2 * chip, 2 * chip + 1] for chip in range(CHIPS)]

    packed = pl.pallas_call(
        pack_kernel,
        out_shape=jax.ShapeDtypeStruct((CHIPS * SLOT, HEAD), jnp.bfloat16),
        in_specs=[VMEM],
        out_specs=VMEM,
        compiler_params=pltpu.CompilerParams(vmem_limit_bytes=8 * 2**20),
        name="pack",
    )(state[0])
    mods = pl.pallas_call(
        pick_kernel,
        out_shape=jax.ShapeDtypeStruct((8 * FRAMES, HEAD), jnp.float32),
        in_specs=[SMEM, ANY],
        out_specs=VMEM,
        scratch_shapes=[
            pltpu.VMEM((COLUMNS, modulation.shape[1], HEAD), jnp.float32),
            pltpu.SemaphoreType.DMA,
        ],
        compiler_params=pltpu.CompilerParams(vmem_limit_bytes=8 * 2**20),
        name="pick",
    )(noise_level, table)
    heads = lax.all_to_all(packed, "frame", 0, 0, axis_index_groups=same_core, tiled=True)
    slots = lax.all_gather(heads, "frame", axis=0, tiled=True, axis_index_groups=same_chip)
    done = pl.pallas_call(
        attend_kernel,
        out_shape=jax.ShapeDtypeStruct((CHIPS * ROWS, HEAD), jnp.bfloat16),
        in_specs=[SMEM, SMEM, VMEM, VMEM],
        out_specs=VMEM,
        scratch_shapes=[
            pltpu.VMEM((2, 8 * CHIPS, ROWS // 8 * HEAD), jnp.float32),
            pltpu.VMEM((2, FRAMES * HALF, HEAD), jnp.float32),
            pltpu.VMEM((FRAMES * 2 * HALF, HEAD), jnp.bfloat16),
            pltpu.VMEM((FRAMES, HEAD + 16, 2 * HALF), jnp.bfloat16),
            pltpu.VMEM((FRAMES // 2, HEAD, 2 * HALF), jnp.bfloat16),
            pltpu.VMEM((20, 2 * HALF, 2 * HALF), jnp.float32),
        ],
        compiler_params=pltpu.CompilerParams(vmem_limit_bytes=24 * 2**20),
        name="attend",
    )(offset, frame_mask, mods, slots)
    back = lax.all_to_all(done, "frame", 0, 0, axis_index_groups=same_core, tiled=True)
    back = back.reshape(FRAMES, PER_FRAME, ROWS, HEAD)[FRAMES - HEADS // PER_FRAME :][::-1]
    rows = jnp.transpose(back.reshape(HEADS, ROWS, HEAD), (1, 0, 2)).reshape(ROWS, WIDTH)
    passed = lax.ppermute(
        rows, "segment", [(i, (i + 1) % segments) for i in range(segments)]
    )
    return passed[None]


def solution(mesh):
    return jax.shard_map(
        body,
        mesh=mesh,
        in_specs=(P("segment", "frame", None), P("segment", None, None, None), P(), P(), P()),
        out_specs=P("segment", "frame", None),
        check_vma=False,
    )
```

time: 62.1 us -> 59.6 us (0.960)
  waiting for transfers between devices: 16.5 us -> 13.9 us
    all_to_all x1, waiting for transfers between devices: 10.3 us -> 7.75 us  [body(): lax.all_to_all(packed, 'frame', 0, 0, axis_index_groups=same_core, tiled=...]
    unnamed x9 -> x10, local copies, waits for them, and re-layouts: 4.03 us -> 4.06 us
where the time goes in v2:
time: 59.6 us; the launch traced here: 59.3 us
  blocking collectives  19.4 us (33%)
  starting transfers between devices  16.2 us (27%)
  waiting for transfers between devices  13.9 us (23%)
  Pallas kernels  4.88 us (8%)
  local copies, waits for them, and re-layouts  4.19 us (7%)
  between operations  0.72 us (1%)
    all_to_all x1, blocking collectives, body(): lax.all_to_all(done, 'frame', 0, 0, axis_index_groups=same_core, tiled=True)  17.1 us
    all_to_all x1, starting transfers between devices, body(): lax.all_to_all(packed, 'frame', 0, 0, axis_index_groups=same_core, tiled=...  13.6 us
    all_to_all x1, waiting for transfers between devices, body(): lax.all_to_all(packed, 'frame', 0, 0, axis_index_groups=same_core, tiled=...  7.75 us
    ppermute x1, waiting for transfers between devices, body(): lax.ppermute(rows, 'segment', [(i, (i + 1) % segments) for i in range(seg...  6.17 us
    unnamed x10, local copies, waits for them, and re-layouts  4.06 us
    pallas_call x1, Pallas kernels, body(): pl.pallas_call(attend_kernel, out_shape=jax.ShapeDtypeStruct((CHIPS * ROW...  3.37 us
    ppermute x1, starting transfers between devices, body(): lax.ppermute(rows, 'segment', [(i, (i + 1) % segments) for i in range(seg...  2.59 us
    all_gather x1, blocking collectives, body(): lax.all_gather(heads, 'frame', axis=0, tiled=True, axis_index_groups=same...  2.26 us
  transfers between devices with their start and end apart: 2, of which 2 were waited for; matrix products, arithmetic and copies ran while one was open for 0% of the time, Pallas kernels for 1%

profile of v2, /device:TPU:32, one launch (start us, length us, event | category | flops | bytes accessed | tf_op | source)
XLA Modules:
  0.0 59.3 jit_solution(4792031075644885897)
XLA Ops:
  0.0 0.0 copy-start.1
  0.0 0.9 %copy-done.1 = bf16[1,32,3072]{2,1,0:T(8,128)(2,1)S(1)} copy-done((bf16[1,32,3072]{2,1,0:T(8,128)(2,1)S(1)}, bf16[1,32,3072]{2,1,0:T(8,128)(2,1)}, u32[]{:S(2)}) %copy-start.1) | copy-done | bytes 196632
  0.9 0.0 copy-start.2
  0.9 0.9 %pack.1 = bf16[1280,128]{1,0:T(8,128)(2,1)} custom-call(bf16[32,3072]{1,0:T(8,128)(2,1)S(1)} %bitcast.18), custom_call_target="tpu_custom_call" | custom-call | tf_op jit(solution)/shard_map/pack/pallas_call | solution.py:197
  1.8 13.6 %all-to-all-start = ((bf16[32,40,128]{2,1,0:T(8,128)(2,1)}), bf16[32,40,128]{2,1,0:T(8,128)(2,1)S(1)}, u32[]{:S(2)}, u32[]{:S(2)}) async-start(bf16[32,40,128]{2,1,0:T(8,128)(2,1)} %bitcast.3), calls=%async_computation | async-start | bytes 655360 | tf_op jit(solution)/shard_map/all_to_all | solution.py:217
  16.0 0.0 copy-start
  16.1 1.8 %copy-done = f32[1,32,7,3072]{3,1,2,0:T(8,128)S(1)} copy-done((f32[1,32,7,3072]{3,1,2,0:T(8,128)S(1)}, f32[1,32,7,3072]{3,1,2,0:T(8,128)}, u32[]{:S(2)}) %copy-start) | copy-done | bytes 2752536
  17.8 0.0 copy-start.3
  17.8 0.7 %copy-done.3 = s32[8]{0:T(128)S(1)} copy-done((s32[8]{0:T(128)S(1)}, s32[8]{0:T(128)}, u32[]{:S(2)}) %copy-start.3) | copy-done | bytes 56
  18.5 0.6 %pick.1.mods = f32[64,128]{1,0:T(8,128)S(1)} custom-call(s32[8]{0:T(128)S(1)} %copy-done.3, f32[7,32,3072]{2,1,0:T(8,128)S(1)} %bitcast.16), custom_call_target="tpu_custom_call" | custom-call | tf_op jit(solution)/shard_map/pick/pallas_call | solution.py:205
  19.1 7.8 %all-to-all-done = bf16[32,40,128]{2,1,0:T(8,128)(2,1)S(1)} async-done(((bf16[32,40,128]{2,1,0:T(8,128)(2,1)}), bf16[32,40,128]{2,1,0:T(8,128)(2,1)S(1)}, u32[]{:S(2)}, u32[]{:S(2)}) %all-to-all-start) | async-done | bytes 327712 | tf_op jit(solution)/shard_map/all_to_all | solution.py:217
  26.9 2.3 %all_gather.3.slots = bf16[2560,128]{1,0:T(8,128)(2,1)S(1)} all-gather(bf16[1280,128]{1,0:T(8,128)(2,1)S(1)} %bitcast.19), channel_id=1, replica_groups={{0,8},{16,24},{32,40},{48,56},{64,72},{80,88},{96,104},{112,120},{128,1..., dimensions={0}, use_global_device_ids=true | all-gather | bytes 983040 | tf_op jit(solution)/shard_map/all_gather | solution.py:218
  29.1 0.0 copy-done.2
  29.1 3.4 %attend.1 = bf16[1024,128]{1,0:T(8,128)(2,1)S(1)} custom-call(s32[1]{0:T(128)S(6)} %copy.11.offset, s32[8,8]{1,0:T(8,128)S(1)} %copy-done.2, f32[64,128]{1,0:T(8,128)S(1)} %pick.1.mods, bf16[2560,128]{1,0:T(8,128)(2,1)S(1)} %all_gather.3.slots), custom_call_target="tpu_custom_call" | custom-call | tf_op jit(solution)/shard_map/attend/pallas_call | solution.py:219
  32.5 17.1 %all_to_all.21 = bf16[32,32,128]{2,1,0:T(8,128)(2,1)S(1)} all-to-all(bf16[32,32,128]{2,1,0:T(8,128)(2,1)S(1)} %bitcast.17), channel_id=1, replica_groups={{448,464,480,496,384,400,416,432,320,336,352,368,256,272,288,304,192,20..., dimensions={0} | all-to-all | bytes 524288 | tf_op jit(solution)/shard_map/all_to_all | solution.py:235
  49.7 0.1 copy.6
  49.8 2.6 %collective-permute-start = (bf16[32,3072]{1,0:T(8,128)(2,1)S(1)}, bf16[32,3072]{1,0:T(8,128)(2,1)S(1)}, u32[]{:S(2)}, u32[]{:S(2)}) collective-permute-start(bf16[32,3072]{1,0:T(8,128)(2,1)S(1)} %bitcast.22), channel_id=1, source_target_pairs={{0,1},{1,2},{2,3},{3,4},{4,5},{5,6},{6,7},{7,0},{8,9},{9,10},{10,1... | collective-permute-start | bytes 589832 | tf_op jit(solution)/shard_map/ppermute | solution.py:238
  52.4 6.2 %collective-permute-done = bf16[32,3072]{1,0:T(8,128)(2,1)S(1)} collective-permute-done((bf16[32,3072]{1,0:T(8,128)(2,1)S(1)}, bf16[32,3072]{1,0:T(8,128)(2,1)S(1)}, u32[]{:S(2)}, u32[]{:S(2)}) %collective-permute-start) | collective-permute-done | bytes 196640 | tf_op jit(solution)/shard_map/ppermute | solution.py:238
  58.6 0.7 %copy.12 = bf16[1,32,3072]{2,1,0:T(8,128)(2,1)} copy(bf16[1,32,3072]{2,1,0:T(8,128)(2,1)S(1)} %bitcast.23) | data formatting | bytes 393216
  (3 shorter events, 0.1 us)
Async XLA Ops:
  0.0 0.9 %copy-start.1 = (bf16[1,32,3072]{2,1,0:T(8,128)(2,1)S(1)}, bf16[1,32,3072]{2,1,0:T(8,128)(2,1)}, u32[]{:S(2)}) copy-start(bf16[1,32,3072]{2,1,0:T(8,128)(2,1)} %param.5) | copy-start | bytes 589828
  0.9 28.2 %copy-start.2 = (s32[8,8]{1,0:T(8,128)S(1)}, s32[8,8]{1,0:T(8,128)}, u32[]{:S(2)}) copy-start(s32[8,8]{1,0:T(8,128)} %mask.1) | copy-start | bytes 772
  1.8 25.0 %all-to-all-start = ((bf16[32,40,128]{2,1,0:T(8,128)(2,1)}), bf16[32,40,128]{2,1,0:T(8,128)(2,1)S(1)}, u32[]{:S(2)}, u32[]{:S(2)}) async-start(bf16[32,40,128]{2,1,0:T(8,128)(2,1)} %bitcast.3), calls=%async_computation | async-start | bytes 655360 | tf_op jit(solution)/shard_map/all_to_all | solution.py:217
  16.0 1.8 %copy-start = (f32[1,32,7,3072]{3,1,2,0:T(8,128)S(1)}, f32[1,32,7,3072]{3,1,2,0:T(8,128)}, u32[]{:S(2)}) copy-start(f32[1,32,7,3072]{3,1,2,0:T(8,128)} %param.6) | copy-start | bytes 8257540
  17.8 0.7 %copy-start.3 = (s32[8]{0:T(128)S(1)}, s32[8]{0:T(128)}, u32[]{:S(2)}) copy-start(s32[8]{0:T(128)} %levels.1) | copy-start | bytes 100
  49.8 8.8 %collective-permute-start = (bf16[32,3072]{1,0:T(8,128)(2,1)S(1)}, bf16[32,3072]{1,0:T(8,128)(2,1)S(1)}, u32[]{:S(2)}, u32[]{:S(2)}) collective-permute-start(bf16[32,3072]{1,0:T(8,128)(2,1)S(1)} %bitcast.22), channel_id=1, source_target_pairs={{0,1},{1,2},{2,3},{3,4},{4,5},{5,6},{6,7},{7,0},{8,9},{9,10},{10,1... | collective-permute-start | bytes 589832 | tf_op jit(solution)/shard_map/ppermute | solution.py:238

commit v3 on v2

--- a/solution.py
+++ b/solution.py
@@ -41,8 +41,7 @@
     for two in range(CHIPS // 2):
         pieces = []
         for slot in (2 * two, 2 * two + 1):
-            chip = PER_FRAME * (FRAMES - 1 - slot // PER_FRAME) + slot % PER_FRAME
-            head = min(chip, HEADS - 1)
+            head = min(CHIPS - 1 - slot, HEADS - 1)
             pieces += [wide[:, HEAD * head : HEAD * (head + 1)], factors]
         both = jnp.concatenate(pieces, axis=0)
         packed[2 * SLOT * two : 2 * SLOT * (two + 1), :] = both.astype(jnp.bfloat16)
@@ -188,10 +187,7 @@
 def body(state, modulation, noise_level, frame_mask, offset):
     segments = lax.axis_size("segment")
     table = jnp.transpose(modulation[0], (1, 0, 2))
-    same_core = [
-        [2 * (PER_FRAME * frame + x) + core for frame in reversed(range(FRAMES)) for x in range(PER_FRAME)]
-        for core in range(2)
-    ]
+    same_core = [[2 * chip + core for chip in reversed(range(CHIPS))] for core in range(2)]
     same_chip = [[2 * chip, 2 * chip + 1] for chip in range(CHIPS)]
 
     packed = pl.pallas_call(
@@ -233,8 +229,8 @@
         name="attend",
     )(offset, frame_mask, mods, slots)
     back = lax.all_to_all(done, "frame", 0, 0, axis_index_groups=same_core, tiled=True)
-    back = back.reshape(FRAMES, PER_FRAME, ROWS, HEAD)[FRAMES - HEADS // PER_FRAME :][::-1]
-    rows = jnp.transpose(back.reshape(HEADS, ROWS, HEAD), (1, 0, 2)).reshape(ROWS, WIDTH)
+    rows = back.reshape(CHIPS, ROWS, HEAD)[CHIPS - HEADS :][::-1]
+    rows = jnp.transpose(rows, (1, 0, 2)).reshape(ROWS, WIDTH)
     passed = lax.ppermute(
         rows, "segment", [(i, (i + 1) % segments) for i in range(segments)]
     )

time: 59.6 us -> 59.4 us (level)
  waiting for transfers between devices: 13.9 us -> 12.5 us
  starting transfers between devices: 16.2 us -> 17.5 us
    all_to_all x1, waiting for transfers between devices: 7.75 us -> 6.35 us  [body(): lax.all_to_all(packed, 'frame', 0, 0, axis_index_groups=same_core, tiled=...]
    all_to_all x1, starting transfers between devices: 13.6 us -> 15 us  [body(): lax.all_to_all(packed, 'frame', 0, 0, axis_index_groups=same_core, tiled=...]
    unnamed x10 -> x9, local copies, waits for them, and re-layouts: 4.06 us -> 4.03 us
where the time goes in v3:
time: 59.4 us; the launch traced here: 59 us
  blocking collectives  19.3 us (32%)
  starting transfers between devices  17.5 us (29%)
  waiting for transfers between devices  12.5 us (21%)
  Pallas kernels  4.89 us (8%)
  local copies, waits for them, and re-layouts  4.06 us (7%)
  between operations  0.7 us (1%)
    all_to_all x1, blocking collectives, body(): lax.all_to_all(done, 'frame', 0, 0, axis_index_groups=same_core, tiled=True)  17 us
    all_to_all x1, starting transfers between devices, body(): lax.all_to_all(packed, 'frame', 0, 0, axis_index_groups=same_core, tiled=...  15 us
    all_to_all x1, waiting for transfers between devices, body(): lax.all_to_all(packed, 'frame', 0, 0, axis_index_groups=same_core, tiled=...  6.35 us
    ppermute x1, waiting for transfers between devices, body(): lax.ppermute(rows, 'segment', [(i, (i + 1) % segments) for i in range(seg...  6.18 us
    unnamed x9, local copies, waits for them, and re-layouts  4.03 us
    pallas_call x1, Pallas kernels, body(): pl.pallas_call(attend_kernel, out_shape=jax.ShapeDtypeStruct((CHIPS * ROW...  3.38 us
    ppermute x1, starting transfers between devices, body(): lax.ppermute(rows, 'segment', [(i, (i + 1) % segments) for i in range(seg...  2.59 us
    all_gather x1, blocking collectives, body(): lax.all_gather(heads, 'frame', axis=0, tiled=True, axis_index_groups=same...  2.26 us
  transfers between devices with their start and end apart: 2, of which 2 were waited for; matrix products, arithmetic and copies ran while one was open for 0% of the time, Pallas kernels for 1%

profile of v3, /device:TPU:32, one launch (start us, length us, event | category | flops | bytes accessed | tf_op | source)
XLA Modules:
  0.0 59.0 jit_solution(4491989951497135896)
XLA Ops:
  0.0 0.0 copy-start.1
  0.0 0.9 %copy-done.1 = bf16[1,32,3072]{2,1,0:T(8,128)(2,1)S(1)} copy-done((bf16[1,32,3072]{2,1,0:T(8,128)(2,1)S(1)}, bf16[1,32,3072]{2,1,0:T(8,128)(2,1)}, u32[]{:S(2)}) %copy-start.1) | copy-done | bytes 196632
  0.9 0.0 copy-start.2
  0.9 0.9 %pack.1 = bf16[1280,128]{1,0:T(8,128)(2,1)} custom-call(bf16[32,3072]{1,0:T(8,128)(2,1)S(1)} %bitcast.16), custom_call_target="tpu_custom_call" | custom-call | tf_op jit(solution)/shard_map/pack/pallas_call | solution.py:193
  1.8 15.0 %all-to-all-start = ((bf16[32,40,128]{2,1,0:T(8,128)(2,1)}), bf16[32,40,128]{2,1,0:T(8,128)(2,1)S(1)}, u32[]{:S(2)}, u32[]{:S(2)}) async-start(bf16[32,40,128]{2,1,0:T(8,128)(2,1)} %bitcast.3), calls=%async_computation | async-start | bytes 655360 | tf_op jit(solution)/shard_map/all_to_all | solution.py:213
  17.4 0.0 copy-start
  17.5 1.8 %copy-done = f32[1,32,7,3072]{3,1,2,0:T(8,128)S(1)} copy-done((f32[1,32,7,3072]{3,1,2,0:T(8,128)S(1)}, f32[1,32,7,3072]{3,1,2,0:T(8,128)}, u32[]{:S(2)}) %copy-start) | copy-done | bytes 2752536
  19.2 0.0 copy-start.3
  19.2 0.7 %copy-done.3 = s32[8]{0:T(128)S(1)} copy-done((s32[8]{0:T(128)S(1)}, s32[8]{0:T(128)}, u32[]{:S(2)}) %copy-start.3) | copy-done | bytes 56
  19.9 0.6 %pick.1.mods = f32[64,128]{1,0:T(8,128)S(1)} custom-call(s32[8]{0:T(128)S(1)} %copy-done.3, f32[7,32,3072]{2,1,0:T(8,128)S(1)} %bitcast.14), custom_call_target="tpu_custom_call" | custom-call | tf_op jit(solution)/shard_map/pick/pallas_call | solution.py:201
  20.5 6.3 %all-to-all-done = bf16[32,40,128]{2,1,0:T(8,128)(2,1)S(1)} async-done(((bf16[32,40,128]{2,1,0:T(8,128)(2,1)}), bf16[32,40,128]{2,1,0:T(8,128)(2,1)S(1)}, u32[]{:S(2)}, u32[]{:S(2)}) %all-to-all-start) | async-done | bytes 327712 | tf_op jit(solution)/shard_map/all_to_all | solution.py:213
  26.9 2.3 %all_gather.3.slots = bf16[2560,128]{1,0:T(8,128)(2,1)S(1)} all-gather(bf16[1280,128]{1,0:T(8,128)(2,1)S(1)} %bitcast.17), channel_id=1, replica_groups={{0,8},{16,24},{32,40},{48,56},{64,72},{80,88},{96,104},{112,120},{128,1..., dimensions={0}, use_global_device_ids=true | all-gather | bytes 983040 | tf_op jit(solution)/shard_map/all_gather | solution.py:214
  29.1 0.0 copy-done.2
  29.1 3.4 %attend.1 = bf16[1024,128]{1,0:T(8,128)(2,1)S(1)} custom-call(s32[1]{0:T(128)S(6)} %copy.10.offset, s32[8,8]{1,0:T(8,128)S(1)} %copy-done.2, f32[64,128]{1,0:T(8,128)S(1)} %pick.1.mods, bf16[2560,128]{1,0:T(8,128)(2,1)S(1)} %all_gather.3.slots), custom_call_target="tpu_custom_call" | custom-call | tf_op jit(solution)/shard_map/attend/pallas_call | solution.py:215
  32.5 17.0 %all_to_all.21 = bf16[32,32,128]{2,1,0:T(8,128)(2,1)S(1)} all-to-all(bf16[32,32,128]{2,1,0:T(8,128)(2,1)S(1)} %bitcast.15), channel_id=1, replica_groups={{496,480,464,448,432,416,400,384,368,352,336,320,304,288,272,256,240,22..., dimensions={0} | all-to-all | bytes 524288 | tf_op jit(solution)/shard_map/all_to_all | solution.py:231
  49.5 2.6 %collective-permute-start = (bf16[32,3072]{1,0:T(8,128)(2,1)S(1)}, bf16[32,3072]{1,0:T(8,128)(2,1)S(1)}, u32[]{:S(2)}, u32[]{:S(2)}) collective-permute-start(bf16[32,3072]{1,0:T(8,128)(2,1)S(1)} %copy_bitcast_fusion), channel_id=1, source_target_pairs={{0,1},{1,2},{2,3},{3,4},{4,5},{5,6},{6,7},{7,0},{8,9},{9,10},{10,1... | collective-permute-start | bytes 589832 | tf_op jit(solution)/shard_map/ppermute | solution.py:234
  52.1 6.2 %collective-permute-done = bf16[32,3072]{1,0:T(8,128)(2,1)S(1)} collective-permute-done((bf16[32,3072]{1,0:T(8,128)(2,1)S(1)}, bf16[32,3072]{1,0:T(8,128)(2,1)S(1)}, u32[]{:S(2)}, u32[]{:S(2)}) %collective-permute-start) | collective-permute-done | bytes 196640 | tf_op jit(solution)/shard_map/ppermute | solution.py:234
  58.3 0.7 %copy.11 = bf16[1,32,3072]{2,1,0:T(8,128)(2,1)} copy(bf16[1,32,3072]{2,1,0:T(8,128)(2,1)S(1)} %bitcast.18) | data formatting | bytes 393216
  (2 shorter events, 0.0 us)
Async XLA Ops:
  0.0 0.9 %copy-start.1 = (bf16[1,32,3072]{2,1,0:T(8,128)(2,1)S(1)}, bf16[1,32,3072]{2,1,0:T(8,128)(2,1)}, u32[]{:S(2)}) copy-start(bf16[1,32,3072]{2,1,0:T(8,128)(2,1)} %param.5) | copy-start | bytes 589828
  0.9 28.2 %copy-start.2 = (s32[8,8]{1,0:T(8,128)S(1)}, s32[8,8]{1,0:T(8,128)}, u32[]{:S(2)}) copy-start(s32[8,8]{1,0:T(8,128)} %mask.1) | copy-start | bytes 772
  1.8 25.0 %all-to-all-start = ((bf16[32,40,128]{2,1,0:T(8,128)(2,1)}), bf16[32,40,128]{2,1,0:T(8,128)(2,1)S(1)}, u32[]{:S(2)}, u32[]{:S(2)}) async-start(bf16[32,40,128]{2,1,0:T(8,128)(2,1)} %bitcast.3), calls=%async_computation | async-start | bytes 655360 | tf_op jit(solution)/shard_map/all_to_all | solution.py:213
  17.4 1.8 %copy-start = (f32[1,32,7,3072]{3,1,2,0:T(8,128)S(1)}, f32[1,32,7,3072]{3,1,2,0:T(8,128)}, u32[]{:S(2)}) copy-start(f32[1,32,7,3072]{3,1,2,0:T(8,128)} %param.6) | copy-start | bytes 8257540
  19.2 0.7 %copy-start.3 = (s32[8]{0:T(128)S(1)}, s32[8]{0:T(128)}, u32[]{:S(2)}) copy-start(s32[8]{0:T(128)} %levels.1) | copy-start | bytes 100
  49.5 8.8 %collective-permute-start = (bf16[32,3072]{1,0:T(8,128)(2,1)S(1)}, bf16[32,3072]{1,0:T(8,128)(2,1)S(1)}, u32[]{:S(2)}, u32[]{:S(2)}) collective-permute-start(bf16[32,3072]{1,0:T(8,128)(2,1)S(1)} %copy_bitcast_fusion), channel_id=1, source_target_pairs={{0,1},{1,2},{2,3},{3,4},{4,5},{5,6},{6,7},{7,0},{8,9},{9,10},{10,1... | collective-permute-start | bytes 589832 | tf_op jit(solution)/shard_map/ppermute | solution.py:234

commit v4 on v3

--- a/solution.py
+++ b/solution.py
@@ -184,6 +184,12 @@
     finish(last_pair)
 
 
+def unpack_kernel(heads, rows):
+    for head in range(HEADS):
+        at = ROWS * (HEADS - 1 - head)
+        rows[:, HEAD * head : HEAD * (head + 1)] = heads[at : at + ROWS, :]
+
+
 def body(state, modulation, noise_level, frame_mask, offset):
     segments = lax.axis_size("segment")
     table = jnp.transpose(modulation[0], (1, 0, 2))
@@ -229,12 +235,20 @@
         name="attend",
     )(offset, frame_mask, mods, slots)
     back = lax.all_to_all(done, "frame", 0, 0, axis_index_groups=same_core, tiled=True)
-    rows = back.reshape(CHIPS, ROWS, HEAD)[CHIPS - HEADS :][::-1]
-    rows = jnp.transpose(rows, (1, 0, 2)).reshape(ROWS, WIDTH)
     passed = lax.ppermute(
-        rows, "segment", [(i, (i + 1) % segments) for i in range(segments)]
+        back[(CHIPS - HEADS) * ROWS :],
+        "segment",
+        [(i, (i + 1) % segments) for i in range(segments)],
     )
-    return passed[None]
+    rows = pl.pallas_call(
+        unpack_kernel,
+        out_shape=jax.ShapeDtypeStruct((ROWS, WIDTH), jnp.bfloat16),
+        in_specs=[VMEM],
+        out_specs=VMEM,
+        compiler_params=pltpu.CompilerParams(vmem_limit_bytes=8 * 2**20),
+        name="unpack",
+    )(passed)
+    return rows[None]
 
 
 def solution(mesh):

time: 59.4 us -> 59.4 us (level)
  the two profiles are of different devices: /device:TPU:32 before, /device:TPU:64 now
where the time goes in v4:
time: 59.4 us; the launch traced here: 59.1 us
  blocking collectives  19.3 us (32%)
  starting transfers between devices  17.5 us (29%)
  waiting for transfers between devices  12.6 us (21%)
  Pallas kernels  5.6 us (9%)
  local copies, waits for them, and re-layouts  3.37 us (6%)
  between operations  0.7 us (1%)
    all_to_all x1, blocking collectives, body(): lax.all_to_all(done, 'frame', 0, 0, axis_index_groups=same_core, tiled=True)  17 us
    all_to_all x1, starting transfers between devices, body(): lax.all_to_all(packed, 'frame', 0, 0, axis_index_groups=same_core, tiled=...  14 us
    all_to_all x1, waiting for transfers between devices, body(): lax.all_to_all(packed, 'frame', 0, 0, axis_index_groups=same_core, tiled=...  6.46 us
    ppermute x1, waiting for transfers between devices, body(): lax.ppermute(back[(CHIPS - HEADS) * ROWS:], 'segment', [(i, (i + 1) % seg...  6.14 us
    ppermute x1, starting transfers between devices, body(): lax.ppermute(back[(CHIPS - HEADS) * ROWS:], 'segment', [(i, (i + 1) % seg...  3.49 us
    pallas_call x1, Pallas kernels, body(): pl.pallas_call(attend_kernel, out_shape=jax.ShapeDtypeStruct((CHIPS * ROW...  3.38 us
    unnamed x8, local copies, waits for them, and re-layouts  3.36 us
    all_gather x1, blocking collectives, body(): lax.all_gather(heads, 'frame', axis=0, tiled=True, axis_index_groups=same...  2.26 us
  transfers between devices with their start and end apart: 2, of which 2 were waited for; matrix products, arithmetic and copies ran while one was open for 0% of the time, Pallas kernels for 1%

profile of v4, /device:TPU:64, one launch (start us, length us, event | category | flops | bytes accessed | tf_op | source)
XLA Modules:
  0.0 59.1 jit_solution(1902286964030628387)
XLA Ops:
  0.0 0.0 copy-start.1
  0.0 0.9 %copy-done.1 = bf16[1,32,3072]{2,1,0:T(8,128)(2,1)S(1)} copy-done((bf16[1,32,3072]{2,1,0:T(8,128)(2,1)S(1)}, bf16[1,32,3072]{2,1,0:T(8,128)(2,1)}, u32[]{:S(2)}) %copy-start.1) | copy-done | bytes 196632
  0.9 0.0 copy-start.2
  0.9 0.9 %pack.1 = bf16[1280,128]{1,0:T(8,128)(2,1)} custom-call(bf16[32,3072]{1,0:T(8,128)(2,1)S(1)} %bitcast.11), custom_call_target="tpu_custom_call" | custom-call | tf_op jit(solution)/shard_map/pack/pallas_call | solution.py:199
  1.8 14.0 %all-to-all-start = ((bf16[32,40,128]{2,1,0:T(8,128)(2,1)}), bf16[32,40,128]{2,1,0:T(8,128)(2,1)S(1)}, u32[]{:S(2)}, u32[]{:S(2)}) async-start(bf16[32,40,128]{2,1,0:T(8,128)(2,1)} %bitcast.3), calls=%async_computation | async-start | bytes 655360 | tf_op jit(solution)/shard_map/all_to_all | solution.py:219
  16.5 0.0 copy-start
  16.5 1.8 %copy-done = f32[1,32,7,3072]{3,1,2,0:T(8,128)S(1)} copy-done((f32[1,32,7,3072]{3,1,2,0:T(8,128)S(1)}, f32[1,32,7,3072]{3,1,2,0:T(8,128)}, u32[]{:S(2)}) %copy-start) | copy-done | bytes 2752536
  18.3 0.0 copy-start.3
  18.3 0.7 %copy-done.3 = s32[8]{0:T(128)S(1)} copy-done((s32[8]{0:T(128)S(1)}, s32[8]{0:T(128)}, u32[]{:S(2)}) %copy-start.3) | copy-done | bytes 56
  18.9 0.6 %pick.1.mods = f32[64,128]{1,0:T(8,128)S(1)} custom-call(s32[8]{0:T(128)S(1)} %copy-done.3, f32[7,32,3072]{2,1,0:T(8,128)S(1)} %bitcast.9), custom_call_target="tpu_custom_call" | custom-call | tf_op jit(solution)/shard_map/pick/pallas_call | solution.py:207
  19.6 6.5 %all-to-all-done = bf16[32,40,128]{2,1,0:T(8,128)(2,1)S(1)} async-done(((bf16[32,40,128]{2,1,0:T(8,128)(2,1)}), bf16[32,40,128]{2,1,0:T(8,128)(2,1)S(1)}, u32[]{:S(2)}, u32[]{:S(2)}) %all-to-all-start) | async-done | bytes 327712 | tf_op jit(solution)/shard_map/all_to_all | solution.py:219
  26.0 2.3 %all_gather.3.slots = bf16[2560,128]{1,0:T(8,128)(2,1)S(1)} all-gather(bf16[1280,128]{1,0:T(8,128)(2,1)S(1)} %bitcast.12), channel_id=1, replica_groups={{0,8},{16,24},{32,40},{48,56},{64,72},{80,88},{96,104},{112,120},{128,1..., dimensions={0}, use_global_device_ids=true | all-gather | bytes 983040 | tf_op jit(solution)/shard_map/all_gather | solution.py:220
  28.3 0.0 copy-done.2
  28.3 3.4 %attend.1 = bf16[1024,128]{1,0:T(8,128)(2,1)S(1)} custom-call(s32[1]{0:T(128)S(6)} %copy.6.offset, s32[8,8]{1,0:T(8,128)S(1)} %copy-done.2, f32[64,128]{1,0:T(8,128)S(1)} %pick.1.mods, bf16[2560,128]{1,0:T(8,128)(2,1)S(1)} %all_gather.3.slots), custom_call_target="tpu_custom_call" | custom-call | tf_op jit(solution)/shard_map/attend/pallas_call | solution.py:221
  31.7 17.0 %all_to_all.21 = bf16[32,32,128]{2,1,0:T(8,128)(2,1)S(1)} all-to-all(bf16[32,32,128]{2,1,0:T(8,128)(2,1)S(1)} %bitcast.10), channel_id=1, replica_groups={{496,480,464,448,432,416,400,384,368,352,336,320,304,288,272,256,240,22..., dimensions={0} | all-to-all | bytes 524288 | tf_op jit(solution)/shard_map/all_to_all | solution.py:237
  48.7 3.5 %collective-permute-start = (bf16[768,128]{1,0:T(8,128)(2,1)S(1)}, bf16[768,128]{1,0:T(8,128)(2,1)S(1)}, u32[]{:S(2)}, u32[]{:S(2)}) collective-permute-start(bf16[768,128]{1,0:T(8,128)(2,1)S(1)} %bitcast.13), channel_id=1, source_target_pairs={{0,1},{1,2},{2,3},{3,4},{4,5},{5,6},{6,7},{7,0},{8,9},{9,10},{10,1... | collective-permute-start | bytes 589832 | tf_op jit(solution)/shard_map/ppermute | solution.py:238
  52.2 6.1 %collective-permute-done.heads = bf16[768,128]{1,0:T(8,128)(2,1)S(1)} collective-permute-done((bf16[768,128]{1,0:T(8,128)(2,1)S(1)}, bf16[768,128]{1,0:T(8,128)(2,1)S(1)}, u32[]{:S(2)}, u32[]{:S(2)}) %collective-permute-start) | collective-permute-done | bytes 196640 | tf_op jit(solution)/shard_map/ppermute | solution.py:238
  58.4 0.7 %unpack.1 = bf16[32,3072]{1,0:T(8,128)(2,1)} custom-call(bf16[768,128]{1,0:T(8,128)(2,1)S(1)} %collective-permute-done.heads), custom_call_target="tpu_custom_call" | custom-call | tf_op jit(solution)/shard_map/unpack/pallas_call | solution.py:243
  (1 shorter events, 0.0 us)
Async XLA Ops:
  0.0 0.9 %copy-start.1 = (bf16[1,32,3072]{2,1,0:T(8,128)(2,1)S(1)}, bf16[1,32,3072]{2,1,0:T(8,128)(2,1)}, u32[]{:S(2)}) copy-start(bf16[1,32,3072]{2,1,0:T(8,128)(2,1)} %param.5) | copy-start | bytes 589828
  0.9 27.4 %copy-start.2 = (s32[8,8]{1,0:T(8,128)S(1)}, s32[8,8]{1,0:T(8,128)}, u32[]{:S(2)}) copy-start(s32[8,8]{1,0:T(8,128)} %mask.1) | copy-start | bytes 772
  1.8 24.2 %all-to-all-start = ((bf16[32,40,128]{2,1,0:T(8,128)(2,1)}), bf16[32,40,128]{2,1,0:T(8,128)(2,1)S(1)}, u32[]{:S(2)}, u32[]{:S(2)}) async-start(bf16[32,40,128]{2,1,0:T(8,128)(2,1)} %bitcast.3), calls=%async_computation | async-start | bytes 655360 | tf_op jit(solution)/shard_map/all_to_all | solution.py:219
  16.5 1.8 %copy-start = (f32[1,32,7,3072]{3,1,2,0:T(8,128)S(1)}, f32[1,32,7,3072]{3,1,2,0:T(8,128)}, u32[]{:S(2)}) copy-start(f32[1,32,7,3072]{3,1,2,0:T(8,128)} %param.6) | copy-start | bytes 8257540
  18.3 0.7 %copy-start.3 = (s32[8]{0:T(128)S(1)}, s32[8]{0:T(128)}, u32[]{:S(2)}) copy-start(s32[8]{0:T(128)} %levels.1) | copy-start | bytes 100
  48.7 9.6 %collective-permute-start = (bf16[768,128]{1,0:T(8,128)(2,1)S(1)}, bf16[768,128]{1,0:T(8,128)(2,1)S(1)}, u32[]{:S(2)}, u32[]{:S(2)}) collective-permute-start(bf16[768,128]{1,0:T(8,128)(2,1)S(1)} %bitcast.13), channel_id=1, source_target_pairs={{0,1},{1,2},{2,3},{3,4},{4,5},{5,6},{6,7},{7,0},{8,9},{9,10},{10,1... | collective-permute-start | bytes 589832 | tf_op jit(solution)/shard_map/ppermute | solution.py:238
